TPU v7x, 32 devices: a whole 2x2x4 slice. The times are simulated.
32 devices in a mesh: grp: 2 (over y), ctx: 1, mdl: 8 (over z, x), dp: 2 (over core).
Axes of the slice: x: 2, y: 2, z: 4, core: 2. Of those that a mesh axis runs over, the one named last changes fastest.
Arguments:
- layer_input: bfloat16 [4, 1024, 2560], P(('grp', 'dp'), 'ctx', 'mdl'), parts along dimension 0, may hold values from -6 to 6
- read_weight: bfloat16 [2560, 128], P('mdl'), may hold values from -0.125 to 0.125
- head_inputs: bfloat16 [4, 1024, 5120], P(('grp', 'dp'), 'ctx', 'mdl'), parts along dimension 0, may hold values from -6 to 6
- write_vectors: bfloat16 [4, 1024, 128], P(('grp', 'dp'), 'ctx'), parts along dimension 0, may hold values from -0.0034179688 to 0.0034179688
- log_decay: float32 [4, 80, 1024], P(('grp', 'dp'), 'mdl', 'ctx'), parts along dimension 0, may hold values from -1 to 0
- segment_ids: int32 [4, 1024], P(('grp', 'dp'), 'ctx'), parts along dimension 0, may hold values from 0 to 3, never falling along the last dimension, each value on 1 to 512 neighbouring positions
- out_grad: bfloat16 [4, 1024, 5120], P(('grp', 'dp'), 'ctx', 'mdl'), parts along dimension 0, may hold values from -0.0029296875 to 0.0029296875
Outputs:
- head_outputs: bfloat16 [4, 1024, 5120], P(('grp', 'dp'), 'ctx', 'mdl'), parts along dimension 0
- read_grad: float32 [256, 2560], P(('grp', 'ctx', 'dp'), 'mdl'), parts along dimension 0
There are 2 independent parts, one for each index of `grp`. A program takes and returns all parts, laid end to end along the dimension named above; an argument that names none is the same for every part. Nothing has to cross between parts.
Inputs may be any that keep to these rules, and one draw needn't show every extreme that they name: `segment_ids`: segment numbers never fall along a trace; each segment is a run of at most 512 positions.
All inputs are finite; a program needn't handle non-finite values.
Results may differ from a plain program's by a relative error of at most 0.015.
Values may be sent and summed in bfloat16 or wider, within the bound.
A program may use at most 64 MiB of HBM per device.

v0:
```python
import jax
import jax.numpy as jnp
from jax import lax
from jax.sharding import PartitionSpec as P

BLOCK_LEN = 512


def shifted(value, axis, by):
    count = lax.axis_size(axis)
    pairs = [(i, i + by) for i in range(count) if 0 <= i + by < count]
    return lax.ppermute(value, axis, pairs)


def join_parts(earlier, later):
    early_first, early_last, early_pass, leading_state = earlier
    later_first, later_last, later_pass, later_state = later
    linked = jnp.logical_or(
        early_last == later_first, jnp.logical_or(early_last < 0.0, later_first < 0.0)
    )
    carried = later_pass * linked.astype(jnp.float32)[..., None]
    front_seg = jnp.where(early_first < 0.0, later_first, early_first)
    back_seg = jnp.where(later_last < 0.0, early_last, later_last)
    return (
        front_seg,
        back_seg,
        early_pass * carried,
        later_state + carried[..., None, None] * leading_state,
    )


def per_device(
    layer_input, read_weight, head_inputs, write_vectors, log_decay, segment_ids, out_grad
):
    trace_count, length, model_cols = layer_input.shape
    head_count = log_decay.shape[1]
    head_dim = head_inputs.shape[2] // head_count
    state_dim = write_vectors.shape[2]
    block_count = length // BLOCK_LEN
    rows_all = trace_count * length
    flat_count = trace_count * block_count
    flat_input = layer_input.reshape(rows_all, model_cols)
    partial_value = jnp.dot(flat_input, read_weight, preferred_element_type=jnp.float32)
    readout = lax.psum(partial_value.astype(jnp.bfloat16), "mdl")
    segments = segment_ids.astype(jnp.float32).reshape(trace_count, block_count, BLOCK_LEN)
    decays = log_decay.reshape(trace_count, head_count, block_count, BLOCK_LEN)
    positions = jnp.arange(BLOCK_LEN)
    cumulative = jnp.cumsum(decays, axis=3)
    closing = cumulative[..., -1:]
    at_end = (segments == segments[..., -1:]).astype(jnp.float32)
    end_weight = jnp.exp(closing - cumulative) * at_end[:, None]
    values = head_inputs.reshape(trace_count, block_count, BLOCK_LEN, head_count, head_dim)
    keys_block = write_vectors.reshape(trace_count, block_count, BLOCK_LEN, state_dim)
    weighted = (values * jnp.transpose(end_weight, (0, 2, 3, 1))[..., None]).astype(jnp.bfloat16)
    block_states = jnp.einsum(
        "bkqhp,bkqn->kbhpn", weighted, keys_block, preferred_element_type=jnp.float32
    )
    front_seg = jnp.transpose(segments[..., 0])
    back_seg = jnp.transpose(segments[..., -1])
    single = (front_seg == back_seg).astype(jnp.float32)
    through = jnp.exp(jnp.transpose(closing[..., 0], (2, 0, 1))) * single[..., None]
    neutral = (
        -jnp.ones((trace_count,), jnp.float32),
        -jnp.ones((trace_count,), jnp.float32),
        jnp.ones((trace_count, head_count), jnp.float32),
        jnp.zeros((trace_count, head_count, head_dim, state_dim), jnp.float32),
    )

    def absorb(running, pieces):
        return (join_parts(running, pieces), running)

    device_total, prefixes = lax.scan(absorb, neutral, (front_seg, back_seg, through, block_states))
    position = lax.axis_index("ctx")

    def relay_once(iteration, incoming):
        outgoing = join_parts(incoming, device_total)
        shifted_lines = shifted((outgoing[0], outgoing[1], outgoing[2], outgoing[3]), "ctx", 1)
        return tuple(
            (
                jnp.where(position == 0, anchor, arrived)
                for anchor, arrived in zip(neutral, shifted_lines)
            )
        )

    entering = lax.fori_loop(0, lax.axis_size("ctx") - 1, relay_once, neutral)
    starts = join_parts(entering, prefixes)
    start_low = starts[3].astype(jnp.bfloat16)
    prior_seg = jnp.transpose(starts[1])
    coupled_items = (segments == prior_seg[..., None]).astype(jnp.float32)
    entry_gain = jnp.exp(cumulative) * coupled_items[:, None]
    gain_rows = jnp.transpose(entry_gain, (0, 2, 3, 1))[..., None]
    readout_block = readout.reshape(trace_count, block_count, BLOCK_LEN, state_dim)
    grads_block = out_grad.reshape(trace_count, block_count, BLOCK_LEN, head_count, head_dim)
    carried_out = (
        jnp.einsum(
            "bkqn,kbhpn->bkqhp", readout_block, start_low, preferred_element_type=jnp.float32
        )
        * gain_rows
    )
    per_head = jnp.einsum(
        "bkqhp,kbhpn->bkqhn", grads_block, start_low, preferred_element_type=jnp.float32
    )
    carried_back = jnp.sum(per_head * gain_rows, axis=3)
    causal = positions[:, None] >= positions[None, :]

    def inside(pieces):
        read_rows, key_rows, value_rows, grad_rows, cum_rows, seg_rows = pieces
        allowed = jnp.logical_and(causal, seg_rows[:, None] == seg_rows[None, :])
        spread = cum_rows[:, :, None] - cum_rows[:, None, :]
        weight = jnp.where(allowed[None], jnp.exp(jnp.where(allowed[None], spread, 0.0)), 0.0)
        scores = jnp.einsum("tn,sn->ts", read_rows, key_rows, preferred_element_type=jnp.float32)
        blend_factor = (weight * scores[None]).astype(jnp.bfloat16)
        inside_out = jnp.einsum(
            "hts,shp->thp", blend_factor, value_rows, preferred_element_type=jnp.float32
        )
        products = jnp.einsum(
            "thp,shp->hts", grad_rows, value_rows, preferred_element_type=jnp.float32
        )
        response = jnp.sum(weight * products, axis=0).astype(jnp.bfloat16)
        inside_back = jnp.dot(response, key_rows, preferred_element_type=jnp.float32)
        return (inside_out, inside_back)

    own_out, own_back = lax.map(
        inside,
        (
            readout_block.reshape(flat_count, BLOCK_LEN, state_dim),
            keys_block.reshape(flat_count, BLOCK_LEN, state_dim),
            values.reshape(flat_count, BLOCK_LEN, head_count, head_dim),
            grads_block.reshape(flat_count, BLOCK_LEN, head_count, head_dim),
            jnp.transpose(cumulative, (0, 2, 1, 3)).reshape(flat_count, head_count, BLOCK_LEN),
            segments.reshape(flat_count, BLOCK_LEN),
        ),
    )
    total_out = (
        own_out.reshape(trace_count, block_count, BLOCK_LEN, head_count, head_dim) + carried_out
    )
    head_outputs = total_out.astype(jnp.bfloat16).reshape(
        trace_count, length, head_count * head_dim
    )
    back_part = (
        own_back.reshape(trace_count, block_count, BLOCK_LEN, state_dim) + carried_back
    ).reshape(rows_all, state_dim)
    read_back = lax.psum(back_part.astype(jnp.bfloat16), "mdl")
    read_grad = lax.psum_scatter(
        lax.dot_general(
            read_back, flat_input, (((0,), (0,)), ((), ())), preferred_element_type=jnp.float32
        ),
        ("ctx", "dp"),
        scatter_dimension=0,
        tiled=True,
    )
    return (head_outputs, read_grad)


def solution(mesh):
    placed = (
        P(("grp", "dp"), "ctx", "mdl"),
        P("mdl", None),
        P(("grp", "dp"), "ctx", "mdl"),
        P(("grp", "dp"), "ctx", None),
        P(("grp", "dp"), "mdl", "ctx"),
        P(("grp", "dp"), "ctx"),
        P(("grp", "dp"), "ctx", "mdl"),
    )
    return jax.shard_map(
        per_device,
        mesh=mesh,
        in_specs=placed,
        out_specs=(P(("grp", "dp"), "ctx", "mdl"), P(("grp", "ctx", "dp"), "mdl")),
        check_vma=False,
    )
```

profile of v0, /device:TPU:0, one launch (start us, length us, event | category | flops | bytes accessed | tf_op | source)
XLA Modules:
  0.0 198.6 jit_solution(15188353820331368359)
XLA Ops:
  7.2 1.0 copy-done
  8.3 2.0 %convolution_convert_fusion = bf16[1024,128]{1,0:T(8,128)(2,1)} fusion(bf16[320,128]{1,0:T(8,128)(2,1)} %param.12, bf16[1,1024,320]{1,2,0:T(8,128)(2,1)S(1)} %copy-done), kind=kOutput, calls=%fused_computation.50 | convolution fusion | flops 84017152 | bytes 999424 | tf_op jit(solution)/shard_map/dot_general | solution.py:43
  11.1 2.3 %reduce-window.6 = f32[1,10,2,4,128]{4,1,2,3,0:T(8,128)S(1)} reduce-window(f32[1,10,2,4,128]{4,1,2,3,0:T(8,128)S(1)} %copy.90, f32[]{:T(128)} %constant.61.clone.1), window={size=1x1x1x1x128 pad=0_0x0_0x0_0x0_0x127_0}, to_apply=%region_1.0 | reduce-window | flops 1300480 | bytes 81924 | tf_op jit(solution)/shard_map/reduce-window
  17.0 2.4 %copy.89 = bf16[1,1024,640]{1,2,0:T(8,128)(2,1)} copy(bf16[1,1024,640]{2,1,0:T(8,128)(2,1)} %param.13) | data formatting | bytes 2621440 | tf_op args[2]
  19.4 3.6 %reshape_reshape.15 = bf16[2,512,10,64]{1,0,3,2:T(2,128)(2,1)S(1)} reshape(bf16[1,1024,640]{1,2,0:T(8,128)(2,1)} %copy.89) | data formatting | bytes 2621440 | tf_op jit(solution)/shard_map/reshape;reshape | solution.py:128
  23.0 1.3 copy.97
  24.3 2.3 %multiply_convert_fusion.6 = bf16[2,512,10,64]{1,0,3,2:T(2,128)(2,1)} fusion(bf16[2,512,10,64]{1,0,3,2:T(2,128)(2,1)S(1)} %reshape_reshape.15, f32[2,512,10]{1,0,2:T(2,128)S(1)} %copy.103), kind=kLoop, calls=%fused_computation.46 | loop fusion | flops 1966080 | bytes 2662400 | tf_op jit(solution)/shard_map/convert_element_type | solution.py:54
  26.7 1.8 fusion.32
  28.6 8.4 %while.40 = (s32[]{:T(128)}, f32[1]{0:T(128)}, f32[1,10]{1,0:T(1,128)S(1)}, f32[1,10,64,128]{3,2,1,0:T(8,128)S(1)}, f32[2,1]{0,1:T(1,128)S(1)}, /*index=5*/f32[2...) while((s32[]{:T(128)}, f32[1]{0:T(128)}, ...), condition=%wide.region_7.8_spmd.clone.clone, body=%wide.region_6.7_spmd.clone.sunk.clone | while | flops 327741 | bytes 1640430 | solution.py:72
  38.1 2.5 %copy.96 = bf16[1,1024,640]{1,2,0:T(8,128)(2,1)} copy(bf16[1,1024,640]{2,1,0:T(8,128)(2,1)} %param.17) | data formatting | bytes 2621440 | tf_op args[6]
  40.6 3.6 %reshape_reshape.19 = bf16[2,512,10,64]{1,0,3,2:T(2,128)(2,1)S(1)} reshape(bf16[1,1024,640]{1,2,0:T(8,128)(2,1)} %copy.96) | data formatting | bytes 2621440 | tf_op jit(solution)/shard_map/reshape;reshape | solution.py:129
  44.4 1.4 copy.99
  45.7 3.0 %fusion.29 = f32[2,512,128]{1,2,0:T(8,128)} fusion(f32[2,512,10]{1,2,0:T(8,128)S(1)} %copy.108, f32[2,1,10,64,128]{4,3,2,1,0:T(8,128)} %get-tuple-element.146, f32[2,10]{1,0:T(2,128)S(1)} %bitcast.194, bf16[2,512,10,64]{1,0,3,2:T(2,128)(2,1)S(1)} %reshape_reshape.19), kind=kOutput, calls=%fused_computation.44 | convolution fusion | flops 170590208 | bytes 2531408 | tf_op jit(solution)/shard_map/bkqhp,kbhpn->bkqhn/dot_general | solution.py:100
  48.7 35.9 %all-reduce.3.cloned.1.call-done = bf16[2,512,128]{2,1,0:T(8,128)(2,1)} async-done(((bf16[2,512,128]{2,1,0:T(8,128)(2,1)}), bf16[2,512,128]{2,1,0:T(8,128)(2,1)}) %all-reduce.3.cloned.1.call-update) | async-done | bytes 262160 | tf_op jit(solution)/shard_map/psum | solution.py:44
  84.7 23.7 %while.39 = (s32[]{:T(128)}, f32[2,512,10,64]{1,3,2,0:T(8,128)}, f32[2,512,128]{1,2,0:T(8,128)}, bf16[2,512,10,64]{1,3,2,0:T(8,128)(2,1)}, f32[2,512]{1,0:T(2,12...) while((s32[]{:T(128)}, f32[2,512,10,64]{1,3,2,0:T(8,128)}, ...), condition=%wide.region_5.6_spmd.clone.clone, body=%wide.region_3.5_spmd.clone.sunk.clone | while | flops 832045056 | bytes 18532508 | solution.py:123
  84.7 1.2 fusion.80
  86.1 5.5 %fusion.82 = f32[2,512,10,64]{1,3,2,0:T(8,128)} fusion(f32[2,512,10,64]{1,3,2,0:T(8,128)} %get-tuple-element.535, s32[]{:T(128)} %get-tuple-element.534, f32[512,512]{1,0:T(8,128)S(1)} %fusion.80, f32[10,512]{1,0:T(8,128)S(1)} %dynamic-slice_bitcast_fusion.3, pred[512,512]{1,0:T(8,128)(4,1)S(1)} %fusion.81, ...), kind=kOutput, calls=%fused_computation.7.clone.1.clone | convolution fusion | flops 348651520 | bytes 3343360 | tf_op jit(solution)/shard_map/while/body/eval_jaxpr/hts,shp->thp/dot_general | solution.py:113
  91.7 3.8 %multiply_reduce_fusion.3 = bf16[512,512]{1,0:T(8,128)(2,1)S(1)} fusion(f32[10,512]{1,0:T(8,128)S(1)} %dynamic-slice_bitcast_fusion.3, pred[512,512]{1,0:T(8,128)(4,1)S(1)} %fusion.81, bf16[2,512,10,64]{1,3,2,0:T(8,128)(2,1)S(1)} %copy-done.5, s32[]{:T(128)} %get-tuple-element.534, bf16[2,512,10,64]{1,3,2,0:T(8,128)(2,1)S(1)} %copy-done.4), kind=kOutput, calls=%fused_computation.1.clone.1.clone | convolution fusion | flops 348389376 | bytes 2163712 | tf_op jit(solution)/shard_map/while/body/eval_jaxpr/thp,shp->hts/dot_general | solution.py:116
  95.5 1.0 fusion.83
  96.5 1.2 fusion.80
  98.0 5.5 %fusion.82 = f32[2,512,10,64]{1,3,2,0:T(8,128)} fusion(f32[2,512,10,64]{1,3,2,0:T(8,128)} %get-tuple-element.535, s32[]{:T(128)} %get-tuple-element.534, f32[512,512]{1,0:T(8,128)S(1)} %fusion.80, f32[10,512]{1,0:T(8,128)S(1)} %dynamic-slice_bitcast_fusion.3, pred[512,512]{1,0:T(8,128)(4,1)S(1)} %fusion.81, ...), kind=kOutput, calls=%fused_computation.7.clone.1.clone | convolution fusion | flops 348651520 | bytes 3343360 | tf_op jit(solution)/shard_map/while/body/eval_jaxpr/hts,shp->thp/dot_general | solution.py:113
  103.5 3.8 %multiply_reduce_fusion.3 = bf16[512,512]{1,0:T(8,128)(2,1)S(1)} fusion(f32[10,512]{1,0:T(8,128)S(1)} %dynamic-slice_bitcast_fusion.3, pred[512,512]{1,0:T(8,128)(4,1)S(1)} %fusion.81, bf16[2,512,10,64]{1,3,2,0:T(8,128)(2,1)S(1)} %copy-done.5, s32[]{:T(128)} %get-tuple-element.534, bf16[2,512,10,64]{1,3,2,0:T(8,128)(2,1)S(1)} %copy-done.4), kind=kOutput, calls=%fused_computation.1.clone.1.clone | convolution fusion | flops 348389376 | bytes 2163712 | tf_op jit(solution)/shard_map/while/body/eval_jaxpr/thp,shp->hts/dot_general | solution.py:116
  107.4 1.0 fusion.83
  108.4 2.1 %add_convert_fusion.2 = bf16[2,512,128]{1,2,0:T(8,128)(2,1)} fusion(f32[2,512,128]{1,2,0:T(8,128)} %get-tuple-element.149, f32[2,512,128]{1,2,0:T(8,128)} %fusion.29), kind=kLoop, calls=%fused_computation.56 | loop fusion | flops 262144 | bytes 1310720 | tf_op jit(solution)/shard_map/convert_element_type | solution.py:143
  110.5 1.8 copy.113
  112.4 70.0 %all-reduce.5.cloned.1.call-done = bf16[1024,128]{1,0:T(8,128)(2,1)} async-done(((bf16[1024,128]{1,0:T(8,128)(2,1)}), bf16[1024,128]{1,0:T(8,128)(2,1)}) %all-reduce.5.cloned.1.call-update) | async-done | bytes 262160 | tf_op jit(solution)/shard_map/psum | solution.py:143
  182.4 2.0 %fusion.35 = f32[128,320]{1,0:T(8,128)} fusion(bf16[1024,128]{1,0:T(8,128)(2,1)} %all-reduce.5.cloned.1.call-done, bf16[1,1024,320]{1,2,0:T(8,128)(2,1)S(1)} %copy-done), kind=kOutput, calls=%fused_computation.51 | convolution fusion | flops 83886080 | bytes 1081344 | tf_op jit(solution)/shard_map/dot_general | solution.py:145
  184.4 1.6 add_convert_fusion
  186.1 1.4 copy.109
  187.4 1.0 reshape.298
  188.4 1.4 copy.114
  189.8 2.3 %reduce-scatter.2.cloned.1.call-done = f32[64,320]{1,0:T(8,128)} async-done(((f32[128,320]{1,0:T(8,128)}), f32[64,320]{1,0:T(8,128)}) %reduce-scatter.2.cloned.1.call-update) | async-done | bytes 81936 | tf_op jit(solution)/shard_map/reduce_scatter | solution.py:144
  (80 shorter events, 9.6 us)
Async XLA Ops:
  7.2 1.1 copy-start
  7.2 77.5 %all-reduce.3.cloned.1.call-start = ((), (), s32[]{:S(2)}) async-start(), calls=%async_computation.1 | async-start | bytes 524288 | tf_op jit(solution)/shard_map/psum | solution.py:44
  10.3 172.1 %all-reduce.5.cloned.1.call-start = ((), (), s32[]{:S(2)}) async-start(), calls=%async_computation.2 | async-start | bytes 524288 | tf_op jit(solution)/shard_map/psum | solution.py:143
  23.0 3.8 %copy-start.1 = (bf16[1,1024,128]{2,1,0:T(8,128)(2,1)S(1)}, bf16[1,1024,128]{2,1,0:T(8,128)(2,1)}, u32[]{:S(2)}) copy-start(bf16[1,1024,128]{2,1,0:T(8,128)(2,1)} %param.14) | copy-start | bytes 786436
  38.1 7.6 %copy-start.6 = (f32[2,512,10]{1,2,0:T(8,128)}, f32[2,512,10]{1,2,0:T(8,128)S(1)}, u32[]{:S(2)}) copy-start(f32[2,512,10]{1,2,0:T(8,128)S(1)} %copy.108) | copy-start | bytes 122884
  86.1 5.5 %copy-start.4 = (bf16[2,512,10,64]{1,3,2,0:T(8,128)(2,1)S(1)}, bf16[2,512,10,64]{1,3,2,0:T(8,128)(2,1)}, u32[]{:S(2)}) copy-start(bf16[2,512,10,64]{1,3,2,0:T(8,128)(2,1)} %get-tuple-element.546) | copy-start | bytes 3932164 | tf_op jit(solution)/shard_map/while
  86.1 5.5 %copy-start.5 = (bf16[2,512,10,64]{1,3,2,0:T(8,128)(2,1)S(1)}, bf16[2,512,10,64]{1,3,2,0:T(8,128)(2,1)}, u32[]{:S(2)}) copy-start(bf16[2,512,10,64]{1,3,2,0:T(8,128)(2,1)} %get-tuple-element.551) | copy-start | bytes 3932164 | tf_op jit(solution)/shard_map/while
  98.0 5.6 %copy-start.4 = (bf16[2,512,10,64]{1,3,2,0:T(8,128)(2,1)S(1)}, bf16[2,512,10,64]{1,3,2,0:T(8,128)(2,1)}, u32[]{:S(2)}) copy-start(bf16[2,512,10,64]{1,3,2,0:T(8,128)(2,1)} %get-tuple-element.546) | copy-start | bytes 3932164 | tf_op jit(solution)/shard_map/while
  98.0 5.5 %copy-start.5 = (bf16[2,512,10,64]{1,3,2,0:T(8,128)(2,1)S(1)}, bf16[2,512,10,64]{1,3,2,0:T(8,128)(2,1)}, u32[]{:S(2)}) copy-start(bf16[2,512,10,64]{1,3,2,0:T(8,128)(2,1)} %get-tuple-element.551) | copy-start | bytes 3932164 | tf_op jit(solution)/shard_map/while
  108.4 76.0 %copy-start.2 = (bf16[2,512,128]{2,1,0:T(8,128)(2,1)S(1)}, bf16[2,512,128]{2,1,0:T(8,128)(2,1)}, u32[]{:S(2)}) copy-start(bf16[2,512,128]{2,1,0:T(8,128)(2,1)} %get-tuple-element.592) | copy-start | bytes 786436
  108.4 76.0 %copy-start.3 = (f32[2,512,10,64]{1,3,2,0:T(8,128)S(1)}, f32[2,512,10,64]{1,3,2,0:T(8,128)}, u32[]{:S(2)}) copy-start(f32[2,512,10,64]{1,3,2,0:T(8,128)} %get-tuple-element.145) | copy-start | bytes 7864324
  112.4 79.7 %reduce-scatter.2.cloned.1.call-start = ((), (), s32[]{:S(2)}) async-start(), calls=%async_computation.3 | async-start | bytes 294912 | tf_op jit(solution)/shard_map/reduce_scatter | solution.py:144
Sparse Core Ops, SparseCore 0:
  11.4 73.2 all-reduce.2
  112.5 69.8 all-reduce.4
  185.2 6.8 reduce-scatter.1
where the time goes:
time: 199 us
  waiting for transfers between devices  108 us (54%)
  matrix products  33.6 us (17%)
  local copies, waits for them, and re-layouts  25.3 us (13%)
  between operations  14 us (7%)
  other arithmetic  12.1 us (6%)
  loops' own time  5.3 us (3%)
    psum x1, waiting for transfers between devices, per_device(): read_back = lax.psum(back_part.astype(jnp.bfloat16), 'mdl')  70 us
    psum x1, waiting for transfers between devices, per_device(): readout = lax.psum(partial_value.astype(jnp.bfloat16), 'mdl')  35.9 us
    dot_general x2, matrix products, inside(): jnp.einsum('hts,shp->thp', blend_factor, value_rows, preferred_element_ty...  11.1 us
    unnamed x19, local copies, waits for them, and re-layouts  10.5 us
    dot_general x2, matrix products, inside(): jnp.einsum('thp,shp->hts', grad_rows, value_rows, preferred_element_type=...  7.62 us
    another operation x1, loops' own time, per_device(): lax.scan(absorb, neutral, (front_seg, back_seg, through, block_states))  5.19 us
  transfers between devices with their start and end apart: 3, of which 3 were waited for; matrix products, arithmetic and copies ran while one was open for 19% of the time, Pallas kernels for 0%

commit v1 on v0

--- a/solution.py
+++ b/solution.py
@@ -41,7 +41,7 @@
     flat_count = trace_count * block_count
     flat_input = layer_input.reshape(rows_all, model_cols)
     partial_value = jnp.dot(flat_input, read_weight, preferred_element_type=jnp.float32)
-    readout = lax.psum(partial_value.astype(jnp.bfloat16), "mdl")
+    readout = jnp.sum(lax.all_gather(partial_value.astype(jnp.bfloat16), "mdl"), axis=0)
     segments = segment_ids.astype(jnp.float32).reshape(trace_count, block_count, BLOCK_LEN)
     decays = log_decay.reshape(trace_count, head_count, block_count, BLOCK_LEN)
     positions = jnp.arange(BLOCK_LEN)

time: 199 us -> 175 us (0.88)
  waiting for transfers between devices: 108 us -> 84.8 us
  matrix products: 33.6 us -> 31.1 us
    psum x1 -> x0, waiting for transfers between devices: 35.9 us -> none  [per_device(): readout = lax.psum(partial_value.astype(jnp.bfloat16), 'mdl')]
    all_gather x0 -> x1, waiting for transfers between devices: none -> 13.9 us  [per_device(): lax.all_gather(partial_value.astype(jnp.bfloat16), 'mdl')]
    unnamed x19 -> x15, local copies, waits for them, and re-layouts: 10.5 us -> 10.5 us
  transfers between devices with their start and end apart: 3 -> 3, of which waited for: 3 -> 3; matrix products, arithmetic and copies ran while one was open for 19% -> 22% of each run, Pallas kernels for 0% -> 0%
where the time goes in v1:
time: 175 us
  waiting for transfers between devices  84.8 us (48%)
  matrix products  31.1 us (18%)
  local copies, waits for them, and re-layouts  26 us (15%)
  between operations  13.9 us (8%)
  other arithmetic  13.4 us (8%)
  loops' own time  5.15 us (3%)
    psum x1, waiting for transfers between devices, per_device(): read_back = lax.psum(back_part.astype(jnp.bfloat16), 'mdl')  69.2 us
    all_gather x1, waiting for transfers between devices, per_device(): lax.all_gather(partial_value.astype(jnp.bfloat16), 'mdl')  13.9 us
    dot_general x2, matrix products, inside(): jnp.einsum('hts,shp->thp', blend_factor, value_rows, preferred_element_ty...  11.1 us
    unnamed x15, local copies, waits for them, and re-layouts  10.5 us
    dot_general x2, matrix products, inside(): jnp.einsum('thp,shp->hts', grad_rows, value_rows, preferred_element_type=...  7.69 us
    another operation x1, loops' own time, per_device(): lax.scan(absorb, neutral, (front_seg, back_seg, through, block_states))  4.79 us
    another operation x1, local copies, waits for them, and re-layouts, per_device(): values.reshape(flat_count, BLOCK_LEN, head_count, head_dim)  3.57 us
    another operation x1, local copies, waits for them, and re-layouts, per_device(): grads_block.reshape(flat_count, BLOCK_LEN, head_count, head_dim)  3.55 us
  transfers between devices with their start and end apart: 3, of which 3 were waited for; matrix products, arithmetic and copies ran while one was open for 22% of the time, Pallas kernels for 0%

profile of v1, /device:TPU:0, one launch (start us, length us, event | category | flops | bytes accessed | tf_op | source)
XLA Modules:
  0.0 174.5 jit_solution(10171443254349821394)
XLA Ops:
  7.2 1.0 copy-done
  8.3 2.0 %convolution_convert_fusion = bf16[1024,128]{1,0:T(8,128)(2,1)} fusion(bf16[320,128]{1,0:T(8,128)(2,1)} %param.12, bf16[1,1024,320]{1,2,0:T(8,128)(2,1)S(1)} %copy-done), kind=kOutput, calls=%fused_computation.50 | convolution fusion | flops 84017152 | bytes 999424 | tf_op jit(solution)/shard_map/dot_general | solution.py:43
  10.3 0.8 copy.90
  11.1 2.3 %reduce-window.6 = f32[1,10,2,4,128]{4,1,2,3,0:T(8,128)S(1)} reduce-window(f32[1,10,2,4,128]{4,1,2,3,0:T(8,128)S(1)} %copy.90, f32[]{:T(128)} %constant.62.clone.1), window={size=1x1x1x1x128 pad=0_0x0_0x0_0x0_0x127_0}, to_apply=%region_1.0 | reduce-window | flops 1300480 | bytes 81924 | tf_op jit(solution)/shard_map/reduce-window
  17.0 2.4 %copy.89 = bf16[1,1024,640]{1,2,0:T(8,128)(2,1)} copy(bf16[1,1024,640]{2,1,0:T(8,128)(2,1)} %param.13) | data formatting | bytes 2621440 | tf_op args[2]
  19.4 3.6 %reshape_reshape.15 = bf16[2,512,10,64]{1,0,3,2:T(2,128)(2,1)S(1)} reshape(bf16[1,1024,640]{1,2,0:T(8,128)(2,1)} %copy.89) | data formatting | bytes 2621440 | tf_op jit(solution)/shard_map/reshape;reshape | solution.py:128
  23.0 1.3 copy.97
  24.3 2.3 %multiply_convert_fusion.6 = bf16[2,512,10,64]{1,0,3,2:T(2,128)(2,1)} fusion(bf16[2,512,10,64]{1,0,3,2:T(2,128)(2,1)S(1)} %reshape_reshape.15, f32[2,512,10]{1,0,2:T(2,128)S(1)} %copy.103), kind=kLoop, calls=%fused_computation.46 | loop fusion | flops 1966080 | bytes 2662400 | tf_op jit(solution)/shard_map/convert_element_type | solution.py:54
  26.7 1.8 %fusion.32 = f32[2,1,10,64,128]{4,3,2,1,0:T(8,128)S(1)} fusion(bf16[2,512,128,1]{2,1,3,0:T(8,128)(2,1)S(1)} %bitcast.182, bf16[2,512,10,64]{1,0,3,2:T(2,128)(2,1)} %multiply_convert_fusion.6), kind=kOutput, calls=%fused_computation.49 | convolution fusion | flops 167772160 | bytes 2228224 | tf_op jit(solution)/shard_map/bkqhp,bkqn->kbhpn/dot_general | solution.py:55
  28.6 8.1 %while.40 = (s32[]{:T(128)}, f32[1]{0:T(128)}, f32[1,10]{1,0:T(1,128)S(1)}, f32[1,10,64,128]{3,2,1,0:T(8,128)S(1)}, f32[2,1]{0,1:T(1,128)S(1)}, /*index=5*/f32[2...) while((s32[]{:T(128)}, f32[1]{0:T(128)}, ...), condition=%wide.region_7.8_spmd.clone.clone, body=%wide.region_6.7_spmd.clone.sunk.clone | while | flops 327741 | bytes 1640430 | solution.py:72
  37.8 2.5 %copy.96 = bf16[1,1024,640]{1,2,0:T(8,128)(2,1)} copy(bf16[1,1024,640]{2,1,0:T(8,128)(2,1)} %param.17) | data formatting | bytes 2621440 | tf_op args[6]
  40.3 3.6 %reshape_reshape.19 = bf16[2,512,10,64]{1,0,3,2:T(2,128)(2,1)S(1)} reshape(bf16[1,1024,640]{1,2,0:T(8,128)(2,1)} %copy.96) | data formatting | bytes 2621440 | tf_op jit(solution)/shard_map/reshape;reshape | solution.py:129
  44.1 1.4 copy.99
  45.5 3.0 %fusion.29 = f32[2,512,128]{1,2,0:T(8,128)} fusion(f32[2,512,10]{1,2,0:T(8,128)S(1)} %copy.108, f32[2,1,10,64,128]{4,3,2,1,0:T(8,128)} %get-tuple-element.146, f32[2,10]{1,0:T(2,128)S(1)} %bitcast.197, bf16[2,512,10,64]{1,0,3,2:T(2,128)(2,1)S(1)} %reshape_reshape.19), kind=kOutput, calls=%fused_computation.44 | convolution fusion | flops 170590208 | bytes 2531408 | tf_op jit(solution)/shard_map/bkqhp,kbhpn->bkqhn/dot_general | solution.py:100
  48.5 13.9 %all-gather.3.cloned.1.call-done = bf16[8192,128]{1,0:T(8,128)(2,1)} async-done(((bf16[1024,128]{1,0:T(8,128)(2,1)}), bf16[8192,128]{1,0:T(8,128)(2,1)}) %all-gather.3.cloned.1.call-update) | async-done | bytes 2097168 | tf_op jit(solution)/shard_map/all_gather | solution.py:44
  62.4 2.0 %reduce_sum.30 = bf16[1024,128]{1,0:T(8,128)(2,1)S(1)} reduce(bf16[8,1024,128]{2,1,0:T(8,128)(2,1)} %bitcast.186, bf16[]{:T(256)} %constant.63.clone.1), dimensions={0}, to_apply=%region_0.0 | reduce | flops 917504 | bytes 2359298 | tf_op jit(solution)/shard_map/reduce_sum | solution.py:44
  64.4 22.4 %while.39 = (s32[]{:T(128)}, f32[2,512,10,64]{1,3,2,0:T(8,128)}, f32[2,512,128]{1,2,0:T(8,128)}, bf16[2,512,10,64]{1,3,2,0:T(8,128)(2,1)}, f32[2,512]{1,0:T(2,12...) while((s32[]{:T(128)}, f32[2,512,10,64]{1,3,2,0:T(8,128)}, ...), condition=%wide.region_5.6_spmd.clone.clone, body=%wide.region_3.5_spmd.clone.sunk.clone | while | flops 832045056 | bytes 22726868 | solution.py:123
  65.2 5.5 %fusion.82 = f32[2,512,10,64]{1,3,2,0:T(8,128)} fusion(f32[2,512,10,64]{1,3,2,0:T(8,128)} %get-tuple-element.535, s32[]{:T(128)} %get-tuple-element.534, f32[512,512]{1,0:T(8,128)S(1)} %fusion.80, f32[10,512]{1,0:T(8,128)S(1)} %dynamic-slice_bitcast_fusion.3, pred[512,512]{1,0:T(8,128)(4,1)S(1)} %fusion.81, ...), kind=kOutput, calls=%fused_computation.7.clone.1.clone | convolution fusion | flops 348651520 | bytes 3343360 | tf_op jit(solution)/shard_map/while/body/eval_jaxpr/hts,shp->thp/dot_general | solution.py:113
  70.7 3.8 %multiply_reduce_fusion.3 = bf16[512,512]{1,0:T(8,128)(2,1)S(1)} fusion(f32[10,512]{1,0:T(8,128)S(1)} %dynamic-slice_bitcast_fusion.3, pred[512,512]{1,0:T(8,128)(4,1)S(1)} %fusion.81, bf16[2,512,10,64]{1,3,2,0:T(8,128)(2,1)S(1)} %copy-done.3, s32[]{:T(128)} %get-tuple-element.534, bf16[2,512,10,64]{1,3,2,0:T(8,128)(2,1)S(1)} %copy-done.2), kind=kOutput, calls=%fused_computation.1.clone.1.clone | convolution fusion | flops 348389376 | bytes 2163712 | tf_op jit(solution)/shard_map/while/body/eval_jaxpr/thp,shp->hts/dot_general | solution.py:116
  74.9 0.8 copy-done.6
  76.3 5.5 %fusion.82 = f32[2,512,10,64]{1,3,2,0:T(8,128)} fusion(f32[2,512,10,64]{1,3,2,0:T(8,128)} %get-tuple-element.535, s32[]{:T(128)} %get-tuple-element.534, f32[512,512]{1,0:T(8,128)S(1)} %fusion.80, f32[10,512]{1,0:T(8,128)S(1)} %dynamic-slice_bitcast_fusion.3, pred[512,512]{1,0:T(8,128)(4,1)S(1)} %fusion.81, ...), kind=kOutput, calls=%fused_computation.7.clone.1.clone | convolution fusion | flops 348651520 | bytes 3343360 | tf_op jit(solution)/shard_map/while/body/eval_jaxpr/hts,shp->thp/dot_general | solution.py:113
  81.8 3.8 %multiply_reduce_fusion.3 = bf16[512,512]{1,0:T(8,128)(2,1)S(1)} fusion(f32[10,512]{1,0:T(8,128)S(1)} %dynamic-slice_bitcast_fusion.3, pred[512,512]{1,0:T(8,128)(4,1)S(1)} %fusion.81, bf16[2,512,10,64]{1,3,2,0:T(8,128)(2,1)S(1)} %copy-done.3, s32[]{:T(128)} %get-tuple-element.534, bf16[2,512,10,64]{1,3,2,0:T(8,128)(2,1)S(1)} %copy-done.2), kind=kOutput, calls=%fused_computation.1.clone.1.clone | convolution fusion | flops 348389376 | bytes 2163712 | tf_op jit(solution)/shard_map/while/body/eval_jaxpr/thp,shp->hts/dot_general | solution.py:116
  86.0 0.8 copy-done.6
  86.8 1.3 add_convert_fusion.2
  88.1 0.8 copy.113
  89.1 69.2 %all-reduce.2.cloned.1.call-done = bf16[1024,128]{1,0:T(8,128)(2,1)} async-done(((bf16[1024,128]{1,0:T(8,128)(2,1)}), bf16[1024,128]{1,0:T(8,128)(2,1)}) %all-reduce.2.cloned.1.call-update) | async-done | bytes 262160 | tf_op jit(solution)/shard_map/psum | solution.py:143
  158.2 2.0 %fusion.35 = f32[128,320]{1,0:T(8,128)} fusion(bf16[1024,128]{1,0:T(8,128)(2,1)} %all-reduce.2.cloned.1.call-done, bf16[1,1024,320]{1,2,0:T(8,128)(2,1)S(1)} %copy-done), kind=kOutput, calls=%fused_computation.51 | convolution fusion | flops 83886080 | bytes 1081344 | tf_op jit(solution)/shard_map/dot_general | solution.py:145
  160.3 2.3 %add_convert_fusion = bf16[2,512,10,64]{1,3,2,0:T(8,128)(2,1)S(1)} fusion(f32[2,512,10,64]{1,3,2,0:T(8,128)} %get-tuple-element.145, bf16[2,512,128,1]{2,1,3,0:T(8,128)(2,1)S(1)} %bitcast.185, f32[2,512,10]{1,2,0:T(8,128)S(1)} %copy.108, f32[2,1,10,64,128]{4,3,2,1,0:T(8,128)S(1)} %copy-done.4, f32[2,10]{1,0:T(2,128)S(1)} %bitcast.198), kind=kOutput, calls=%fused_computation.45 | convolution fusion | flops 170065920 | bytes 4890704 | tf_op jit(solution)/shard_map/bkqn,kbhpn->bkqhp/dot_general | solution.py:95
  162.5 1.4 copy.109
  163.9 1.0 reshape.298
  164.9 1.4 copy.114
  166.3 1.7 reduce-scatter.2.cloned.1.call-done
  (85 shorter events, 10.1 us)
Async XLA Ops:
  7.2 1.1 copy-start
  7.2 55.2 %all-gather.3.cloned.1.call-start = ((), (), s32[]{:S(2)}) async-start(), calls=%async_computation.3 | async-start | bytes 2359296 | tf_op jit(solution)/shard_map/all_gather | solution.py:44
  10.3 147.9 %all-reduce.2.cloned.1.call-start = ((), (), s32[]{:S(2)}) async-start(), calls=%async_computation.1 | async-start | bytes 524288 | tf_op jit(solution)/shard_map/psum | solution.py:143
  23.0 3.7 %copy-start.1 = (bf16[1,1024,128]{2,1,0:T(8,128)(2,1)S(1)}, bf16[1,1024,128]{2,1,0:T(8,128)(2,1)}, u32[]{:S(2)}) copy-start(bf16[1,1024,128]{2,1,0:T(8,128)(2,1)} %param.14) | copy-start | bytes 786436
  65.2 5.6 %copy-start.2 = (bf16[2,512,10,64]{1,3,2,0:T(8,128)(2,1)S(1)}, bf16[2,512,10,64]{1,3,2,0:T(8,128)(2,1)}, u32[]{:S(2)}) copy-start(bf16[2,512,10,64]{1,3,2,0:T(8,128)(2,1)} %get-tuple-element.546) | copy-start | bytes 3932164 | tf_op jit(solution)/shard_map/while
  65.2 5.5 %copy-start.3 = (bf16[2,512,10,64]{1,3,2,0:T(8,128)(2,1)S(1)}, bf16[2,512,10,64]{1,3,2,0:T(8,128)(2,1)}, u32[]{:S(2)}) copy-start(bf16[2,512,10,64]{1,3,2,0:T(8,128)(2,1)} %get-tuple-element.551) | copy-start | bytes 3932164 | tf_op jit(solution)/shard_map/while
  70.7 3.9 %copy-start.5 = (f32[2,512,128]{1,2,0:T(8,128)S(1)}, f32[2,512,128]{1,2,0:T(8,128)}, u32[]{:S(2)}) copy-start(f32[2,512,128]{1,2,0:T(8,128)} %get-tuple-element.536) | copy-start | bytes 1572868 | tf_op jit(solution)/shard_map/while
  74.9 0.8 copy-start.6
  76.2 5.6 %copy-start.2 = (bf16[2,512,10,64]{1,3,2,0:T(8,128)(2,1)S(1)}, bf16[2,512,10,64]{1,3,2,0:T(8,128)(2,1)}, u32[]{:S(2)}) copy-start(bf16[2,512,10,64]{1,3,2,0:T(8,128)(2,1)} %get-tuple-element.546) | copy-start | bytes 3932164 | tf_op jit(solution)/shard_map/while
  76.3 5.6 %copy-start.3 = (bf16[2,512,10,64]{1,3,2,0:T(8,128)(2,1)S(1)}, bf16[2,512,10,64]{1,3,2,0:T(8,128)(2,1)}, u32[]{:S(2)}) copy-start(bf16[2,512,10,64]{1,3,2,0:T(8,128)(2,1)} %get-tuple-element.551) | copy-start | bytes 3932164 | tf_op jit(solution)/shard_map/while
  81.8 3.9 %copy-start.5 = (f32[2,512,128]{1,2,0:T(8,128)S(1)}, f32[2,512,128]{1,2,0:T(8,128)}, u32[]{:S(2)}) copy-start(f32[2,512,128]{1,2,0:T(8,128)} %get-tuple-element.536) | copy-start | bytes 1572868 | tf_op jit(solution)/shard_map/while
  86.0 0.8 copy-start.6
  86.8 73.4 %copy-start.4 = (f32[2,1,10,64,128]{4,3,2,1,0:T(8,128)S(1)}, f32[2,1,10,64,128]{4,3,2,1,0:T(8,128)}, u32[]{:S(2)}) copy-start(f32[2,1,10,64,128]{4,3,2,1,0:T(8,128)} %get-tuple-element.146) | copy-start | bytes 1966084
  89.0 79.0 %reduce-scatter.2.cloned.1.call-start = ((), (), s32[]{:S(2)}) async-start(), calls=%async_computation.2 | async-start | bytes 294912 | tf_op jit(solution)/shard_map/reduce_scatter | solution.py:144
Sparse Core Ops, SparseCore 0:
  10.4 51.9 all-gather.2
  89.1 69.0 all-reduce.1
  161.1 6.8 reduce-scatter.1
